TPU v7x, 32 devices: a whole 2x2x4 slice. The times are simulated.
32 devices in a mesh: rep: 4 (over y, x), blk: 8 (over z, core).
Axes of the slice: x: 2, y: 2, z: 4, core: 2. Of those that a mesh axis runs over, the one named last changes fastest.
Arguments:
- features: bfloat16 [8, 2048, 128], P('blk', 'rep'), may hold values from -6 to 6
- weight: bfloat16 [128, 256], replicated, may hold values from -0.5 to 0.5
- cotangent: bfloat16 [8, 2048, 256], P('blk', 'rep'), may hold values from -6 to 6
- self_weight: float32 [8, 2048], P('blk', 'rep'), may hold values from 0.3 to 1.5
- block_rows: int32 [4, 8, 384], P('rep', 'blk'), may hold values from 0 to 31, as said below
- block_cols: int32 [4, 8, 384], P('rep', 'blk'), may hold values from 0 to 15, as said below
- block_counts: int32 [4, 8], P('rep', 'blk'), may hold values from 1 to 384, as said below
- block_values: bfloat16 [4, 8, 384, 128, 128], P('rep', 'blk'), as said below
Outputs:
- activated: bfloat16 [8, 2048, 256], P('blk', 'rep')
- feature_grad: bfloat16 [8, 2048, 128], P('blk', 'rep')
- weight_grad: float32 [128, 256], P('rep')
Inputs may be any that keep to these rules, and one draw needn't show every extreme that they name: `block_counts`: one device of every draw has all 384 slots live. `block_rows`: the live slots of one device name distinct (row tile, column tile) pairs; slots past the count hold 0. `block_cols`: slots past the count hold 0. `block_values`: slots at or past a device's count hold zeros.
All inputs are finite; a program needn't handle non-finite values.
Results may differ from a plain program's by a relative error of at most 0.024.
Values may be sent and summed in bfloat16 or wider, within the bound.
A program may use at most 128 MiB of HBM per device.

v0:
```python
import math

import jax
import jax.numpy as jnp
from jax import lax
from jax.sharding import PartitionSpec as P

group_slots = 32


def silu_slope(pre_act):
    sigma = jax.nn.sigmoid(pre_act)
    return sigma * (1.0 + pre_act * (1.0 - sigma))


def tile_products(tile_values, row_index, col_index, live_count, source, targets, flipped):
    feat_width = source.shape[-1]
    tile_side = tile_values.shape[-1]
    start_sums = jnp.zeros((targets, tile_side, feat_width), jnp.float32)
    turn_count = (live_count + group_slots - 1) // group_slots

    def one_group(step_index, summed):
        first_slot = step_index * group_slots
        tile_block = lax.dynamic_slice_in_dim(tile_values, first_slot, group_slots, 0)
        rows_here = lax.dynamic_slice_in_dim(row_index, first_slot, group_slots, 0)
        cols_here = lax.dynamic_slice_in_dim(col_index, first_slot, group_slots, 0)
        is_live = (first_slot + jnp.arange(group_slots, dtype=jnp.int32) < live_count).astype(
            jnp.float32
        )
        if flipped:
            picked = source[rows_here]
            products = jnp.einsum(
                "gji,gjf->gif", tile_block, picked, preferred_element_type=jnp.float32
            )
            landing = cols_here
        else:
            picked = source[cols_here]
            products = jnp.einsum(
                "gij,gjf->gif", tile_block, picked, preferred_element_type=jnp.float32
            )
            landing = rows_here
        return summed.at[landing].add(products * is_live[:, None, None])

    return lax.fori_loop(0, turn_count, one_group, start_sums)


def on_device(
    features, weight, cotangent, self_weight, block_rows, block_cols, block_counts, block_values
):
    rows_dev = features.shape[1]
    feat_width = features.shape[2]
    tile_side = block_values.shape[-1]
    blk_count = lax.axis_size("blk")
    rep_count = lax.axis_size("rep")
    tile_values = block_values[0, 0]
    row_index = block_rows[0, 0]
    col_index = block_cols[0, 0]
    live_count = block_counts[0, 0]
    row_tiles = blk_count * rows_dev // tile_side
    col_tiles = rep_count * rows_dev // tile_side
    panel = lax.all_gather(features, "rep", axis=1, tiled=True)
    panel_tiles = panel.reshape(col_tiles, tile_side, feat_width)
    own_scale = self_weight[0][:, None]
    forward_terms = tile_products(
        tile_values, row_index, col_index, live_count, panel_tiles, row_tiles, False
    )
    forward_terms = forward_terms.reshape(blk_count, rows_dev, feat_width)
    summed_rows = lax.psum_scatter(
        forward_terms.astype(jnp.bfloat16), "blk", scatter_dimension=0, tiled=True
    ).astype(jnp.float32)[0]
    aggregated = (summed_rows + own_scale * features[0].astype(jnp.float32)).astype(jnp.bfloat16)
    pre_act = jnp.dot(aggregated, weight, preferred_element_type=jnp.float32)
    activated = jax.nn.silu(pre_act).astype(jnp.bfloat16)
    slope = (cotangent[0].astype(jnp.float32) * silu_slope(pre_act)).astype(jnp.bfloat16)
    node_total = blk_count * rep_count * rows_dev
    weight_part = jnp.einsum(
        "nf,nh->fh", aggregated, slope, preferred_element_type=jnp.float32
    ) / math.sqrt(node_total)
    row_grad = lax.dot_general(
        slope, weight, (((1,), (1,)), ((), ())), preferred_element_type=jnp.float32
    ).astype(jnp.bfloat16)
    all_grads = lax.all_gather(row_grad[None], "blk", axis=0, tiled=True)
    grad_tiles = all_grads.reshape(row_tiles, tile_side, feat_width)
    backward_terms = tile_products(
        tile_values, row_index, col_index, live_count, grad_tiles, col_tiles, True
    )
    backward_terms = backward_terms.reshape(1, rep_count * rows_dev, feat_width)
    own_grad = own_scale * row_grad.astype(jnp.float32)
    column_part = lax.psum_scatter(
        backward_terms.astype(jnp.bfloat16), "rep", scatter_dimension=1, tiled=True
    ).astype(jnp.float32)
    weight_full = lax.psum(weight_part, ("rep", "blk"))
    share_rows = weight_full.shape[0] // rep_count
    weight_grad = lax.dynamic_slice_in_dim(
        weight_full, lax.axis_index("rep") * share_rows, share_rows, 0
    )
    feature_grad = (column_part[0] + own_grad).astype(jnp.bfloat16)
    return (activated[None], feature_grad[None], weight_grad)


def solution(mesh):
    placed = (
        P("blk", "rep", None),
        P(),
        P("blk", "rep", None),
        P("blk", "rep"),
        P("rep", "blk", None),
        P("rep", "blk", None),
        P("rep", "blk"),
        P("rep", "blk", None, None, None),
    )
    return jax.shard_map(
        on_device,
        mesh=mesh,
        in_specs=placed,
        out_specs=(P("blk", "rep", None), P("blk", "rep", None), P("rep", None)),
        check_vma=False,
    )
```

profile of v0, /device:TPU:0, one launch (start us, length us, event | category | flops | bytes accessed | tf_op | source)
XLA Modules:
  0.0 368.8 jit_solution(2766912742869231997)
XLA Ops:
  7.9 0.7 reduce
  8.6 0.7 reduce.1
  9.3 13.1 %all_gather.6 = bf16[1,2048,128]{2,1,0:T(8,128)(2,1)} all-gather(bf16[1,512,128]{2,1,0:T(8,128)(2,1)} %param.12), channel_id=1, replica_groups=mesh['rep'=4,'blk'=8] {'rep'}, dimensions={1}, use_global_device_ids=true | all-gather | bytes 655360 | tf_op jit(solution)/shard_map/all_gather | solution.py:61
  22.4 1.6 broadcast_in_dim.29
  24.0 31.1 %while.20 = (s32[]{:T(128)}, f32[32,128,128]{2,1,0:T(8,128)}, s32[]{:T(128)}, s32[384]{0:T(512)S(1)}, bf16[384,128,128]{2,1,0:T(8,128)(2,1)}, /*index=5*/s32[384...) while((s32[]{:T(128)}, f32[32,128,128]{2,1,0:T(8,128)}, ...), condition=%wide.region_2.3_spmd, body=%wide.region_0.2_spmd.sunk | while | flops 135267616 | bytes 12588339 | solution.py:44
  24.0 0.6 compare_convert_fusion.4
  24.7 0.1 compare_select_fusion.6
  24.7 1.8 gather_fusion
  26.5 1.7 convolution_multiply_fusion.5
  28.2 6.1 %scatter_fusion = f32[32,128,128]{2,1,0:T(8,128)} fusion(f32[32,128,128]{2,1,0:T(8,128)} %get-tuple-element.258, s32[32]{0:T(128)S(1)} %get-tuple-element.233, f32[32,128,128]{2,1,0:T(8,128)S(1)} %convolution_multiply_fusion.5), kind=kCustom, calls=%fused_computation.2.clone.1 | custom fusion | flops 524288 | bytes 6291584 | tf_op jit(solution)/shard_map/while/body/scatter-add | solution.py:42
  34.3 0.6 compare_convert_fusion.4
  35.0 0.1 compare_select_fusion.6
  35.1 1.8 gather_fusion
  36.9 1.7 convolution_multiply_fusion.5
  38.6 6.1 %scatter_fusion = f32[32,128,128]{2,1,0:T(8,128)} fusion(f32[32,128,128]{2,1,0:T(8,128)} %get-tuple-element.258, s32[32]{0:T(128)S(1)} %get-tuple-element.233, f32[32,128,128]{2,1,0:T(8,128)S(1)} %convolution_multiply_fusion.5), kind=kCustom, calls=%fused_computation.2.clone.1 | custom fusion | flops 524288 | bytes 6291584 | tf_op jit(solution)/shard_map/while/body/scatter-add | solution.py:42
  44.7 0.6 compare_convert_fusion.4
  45.4 1.8 gather_fusion
  47.2 1.7 convolution_multiply_fusion.5
  48.9 6.2 %scatter_fusion = f32[32,128,128]{2,1,0:T(8,128)} fusion(f32[32,128,128]{2,1,0:T(8,128)} %get-tuple-element.258, s32[32]{0:T(128)S(1)} %get-tuple-element.233, f32[32,128,128]{2,1,0:T(8,128)S(1)} %convolution_multiply_fusion.5), kind=kCustom, calls=%fused_computation.2.clone.1 | custom fusion | flops 524288 | bytes 6291584 | tf_op jit(solution)/shard_map/while/body/scatter-add | solution.py:42
  55.1 2.8 convert_element_type.66
  58.0 124.9 %reduce-scatter.3.cloned.1.call-done = bf16[1,512,128]{2,1,0:T(8,128)(2,1)} async-done(((bf16[8,512,128]{2,1,0:T(8,128)(2,1)}), bf16[1,512,128]{2,1,0:T(8,128)(2,1)}) %reduce-scatter.3.cloned.1.call-update) | async-done | bytes 131088 | tf_op jit(solution)/shard_map/reduce_scatter | solution.py:68
  182.9 2.1 fusion.4
  185.0 0.9 convolution_convert_fusion
  186.0 16.7 %copy.11 = bf16[1,1,384,128,128]{3,4,2,1,0:T(8,128)(2,1)} copy(bf16[1,1,384,128,128]{4,3,2,1,0:T(8,128)(2,1)} %bitcast.45) | data formatting | bytes 25165824 | tf_op args[7]
  202.7 1.0 convolution_multiply_fusion.2
  203.7 2.6 all-gather.3.cloned.1.call-done
  206.3 0.1 broadcast_in_dim.31
  206.4 24.9 %while.21 = (s32[]{:T(128)}, f32[16,128,128]{2,1,0:T(8,128)S(1)}, s32[]{:T(128)}, s32[384]{0:T(512)S(1)}, bf16[384,128,128]{1,2,0:T(8,128)(2,1)}, /*index=5*/s32...) while((s32[]{:T(128)}, f32[16,128,128]{2,1,0:T(8,128)S(1)}, ...), condition=%wide.region_6.7_spmd, body=%wide.region_4.6_spmd.sunk | while | flops 135267616 | bytes 12588339 | solution.py:44
  206.4 0.7 compare_convert_fusion.5
  207.1 0.1 compare_select_fusion.7
  207.2 2.9 gather_fusion.1
  210.1 2.0 convolution_multiply_fusion.6
  212.0 2.7 scatter_fusion.1
  214.7 0.7 compare_convert_fusion.5
  215.4 0.1 compare_select_fusion.7
  215.5 2.9 gather_fusion.1
  218.4 2.0 convolution_multiply_fusion.6
  220.3 2.7 scatter_fusion.1
  223.0 0.7 compare_convert_fusion.5
  223.7 0.1 compare_select_fusion.7
  223.8 2.9 gather_fusion.1
  226.7 2.0 convolution_multiply_fusion.6
  228.6 2.7 scatter_fusion.1
  231.3 0.9 convert_element_type.76
  232.3 101.7 %all-reduce.2.cloned.1.call-done = f32[128,256]{1,0:T(8,128)} async-done(((f32[128,256]{1,0:T(8,128)}), f32[128,256]{1,0:T(8,128)}) %all-reduce.2.cloned.1.call-update) | async-done | bytes 131088 | tf_op jit(solution)/shard_map/psum | solution.py:92
  334.0 1.4 constant_dynamic-slice_fusion
  335.4 25.2 %reduce-scatter.5.cloned.1.call-done = bf16[1,512,128]{2,1,0:T(8,128)(2,1)} async-done(((bf16[1,2048,128]{2,1,0:T(8,128)(2,1)}), bf16[1,512,128]{2,1,0:T(8,128)(2,1)}) %reduce-scatter.5.cloned.1.call-update) | async-done | bytes 131088 | tf_op jit(solution)/shard_map/reduce_scatter | solution.py:89
  360.5 1.7 fusion.9
  (27 shorter events, 0.4 us)
Async XLA Ops:
  7.2 175.8 %copy-start = (bf16[128,256]{1,0:T(8,128)(2,1)S(1)}, bf16[128,256]{1,0:T(8,128)(2,1)}, u32[]{:S(2)}) copy-start(bf16[128,256]{1,0:T(8,128)(2,1)} %param.13) | copy-start | bytes 196612
  7.2 175.8 %reduce-scatter.3.cloned.1.call-start = ((), (), s32[]{:S(2)}) async-start(), calls=%async_computation.2 | async-start | bytes 1179648 | tf_op jit(solution)/shard_map/reduce_scatter | solution.py:68
  55.1 127.8 %copy-start.2 = (bf16[1,512,128]{2,1,0:T(8,128)(2,1)S(1)}, bf16[1,512,128]{2,1,0:T(8,128)(2,1)}, u32[]{:S(2)}) copy-start(bf16[1,512,128]{2,1,0:T(8,128)(2,1)} %param.12) | copy-start | bytes 393220
  55.1 127.8 %copy-start.4 = (f32[1,512]{1,0:T(1,128)S(1)}, f32[1,512]{1,0:T(1,128)}, u32[]{:S(2)}) copy-start(f32[1,512]{1,0:T(1,128)} %param.15) | copy-start | bytes 6148
  55.1 127.8 %copy-start.5 = (bf16[1,512,256]{2,1,0:T(8,128)(2,1)S(1)}, bf16[1,512,256]{2,1,0:T(8,128)(2,1)}, u32[]{:S(2)}) copy-start(bf16[1,512,256]{2,1,0:T(8,128)(2,1)} %param.14) | copy-start | bytes 786436
  58.0 148.3 %all-gather.3.cloned.1.call-start = ((), (), s32[]{:S(2)}) async-start(), calls=%async_computation.5 | async-start | bytes 1179648 | tf_op jit(solution)/shard_map/all_gather | solution.py:82
  185.9 148.1 %all-reduce.2.cloned.1.call-start = ((), (), s32[]{:S(2)}) async-start(), calls=%async_computation.4 | async-start | bytes 262144 | tf_op jit(solution)/shard_map/psum | solution.py:92
  186.0 16.7 %copy-start.3 = (bf16[1,512,128]{2,1,0:T(8,128)(2,1)S(1)}, bf16[1,512,128]{2,1,0:T(8,128)(2,1)}, u32[]{:S(2)}) copy-start(bf16[1,512,128]{2,1,0:T(8,128)(2,1)} %reduce-scatter.3.cloned.1.call-done) | copy-start | bytes 393220
  203.7 156.8 %reduce-scatter.5.cloned.1.call-start = ((), (), s32[]{:S(2)}) async-start(), calls=%async_computation.3 | async-start | bytes 655360 | tf_op jit(solution)/shard_map/reduce_scatter | solution.py:89
  231.3 129.2 %copy-start.1 = (bf16[512,128]{1,0:T(8,128)(2,1)S(1)}, bf16[512,128]{1,0:T(8,128)(2,1)}, u32[]{:S(2)}) copy-start(bf16[512,128]{1,0:T(8,128)(2,1)} %convolution_convert_fusion) | copy-start | bytes 393220
Sparse Core Ops, SparseCore 0:
  58.1 124.7 reduce-scatter.2
  186.0 20.2 all-gather.2
  211.8 122.0 all-reduce.1
  336.7 23.8 reduce-scatter.4
where the time goes:
time: 372 us; the launch traced here: 369 us
  waiting for transfers between devices  254 us (68%)
  other arithmetic  37.7 us (10%)
  local copies, waits for them, and re-layouts  33.8 us (9%)
  matrix products  14.8 us (4%)
  between operations  14.5 us (4%)
  blocking collectives  13.1 us (4%)
    reduce_scatter x1, waiting for transfers between devices, on_device(): lax.psum_scatter(forward_terms.astype(jnp.bfloat16), 'blk', scatter_dimen...  125 us
    psum x1, waiting for transfers between devices, on_device(): weight_full = lax.psum(weight_part, ('rep', 'blk'))  102 us
    scatter-add x6, other arithmetic, one_group(): return summed.at[landing].add(products * is_live[:, None, None])  26.5 us
    reduce_scatter x1, waiting for transfers between devices, on_device(): lax.psum_scatter(backward_terms.astype(jnp.bfloat16), 'rep', scatter_dime...  25.2 us
    unnamed x13, local copies, waits for them, and re-layouts  16.7 us
    all_gather x1, blocking collectives, on_device(): panel = lax.all_gather(features, 'rep', axis=1, tiled=True)  13.1 us
    gather x3, local copies, waits for them, and re-layouts, one_group(): picked = source[rows_here]  8.66 us
  transfers between devices with their start and end apart: 4, of which 4 were waited for; matrix products, arithmetic and copies ran while one was open for 12% of the time, Pallas kernels for 0%

commit v1 on v0

--- a/solution.py
+++ b/solution.py
@@ -1,8 +1,11 @@
+import functools
 import math
 
 import jax
 import jax.numpy as jnp
 from jax import lax
+from jax.experimental import pallas as pl
+from jax.experimental.pallas import tpu as pltpu
 from jax.sharding import PartitionSpec as P
 
 group_slots = 32
@@ -44,7 +47,299 @@
     return lax.fori_loop(0, turn_count, one_group, start_sums)
 
 
-def on_device(
+cores = 2
+load_parts = 8
+dense_limit = 20 * 2**20
+vmem_bytes = 52 * 2**20
+MESH = pl.DeviceIdType.MESH
+
+
+def flip(place, mask):
+    bit = 1
+    while bit <= mask:
+        if mask & bit:
+            place = place + bit - 2 * bit * lax.rem(lax.div(place, bit), 2)
+        bit *= 2
+    return place
+
+
+def layer_kernel(
+    n_rep, n_blk, inv_root,
+    slot_ref, x_ref, w_ref, cot_ref, scale_ref, values_ref,
+    act_ref, fgrad_ref, wgrad_ref,
+    tiles, dense, panel, pair_out, pair_in, line_out, line_in, agg_ref, slope_ref,
+    grads, sums, col_out, col_in, w_part, w_in, w_pair_out, w_pair_in, w_line_out, w_line_in,
+    tile_sem, feat_sem, pair_sem, line_sem, grad_line_sem, grad_pair_sem, col_sem,
+    w_rep_sem, w_pair_sem, w_line_sem,
+):
+    rep = lax.axis_index("rep")
+    blk = lax.axis_index("blk")
+    z = lax.div(blk, cores)
+    core = lax.rem(blk, cores)
+    n_z = n_blk // cores
+    cap, side, _ = values_ref.shape
+    rows, feat = x_ref.shape
+    col_tiles = n_rep * rows // side
+    tiles_per_block = rows // side
+    f32, bf16 = jnp.float32, jnp.bfloat16
+    pair = (rep, blk + 1 - 2 * core)
+
+    def line(mask):
+        return flip(z, mask) * cores + core
+
+    pending = []
+
+    def send(source, target, sems, at, device):
+        copy = pltpu.make_async_remote_copy(
+            src_ref=source, dst_ref=target,
+            send_sem=sems.at[0, at], recv_sem=sems.at[1, at],
+            device_id=device, device_id_type=MESH,
+        )
+        copy.start()
+        pending.append(copy)
+        return copy
+
+    part = cap // load_parts
+    loads = []
+    for k in range(load_parts):
+        piece = pl.ds(k * part, part)
+        load = pltpu.make_async_copy(values_ref.at[piece], tiles.at[piece], tile_sem.at[k])
+        load.start()
+        loads.append(load)
+    tiles[cap] = jnp.zeros((side, side), bf16)
+    panel[rep] = x_ref[...]
+
+    partners = [(flip(rep, m), blk) for m in range(1, n_rep)]
+    partners += [(rep, line(m)) for m in range(1, n_z)]
+    partners += [pair]
+    barrier = pltpu.get_barrier_semaphore()
+    for device in partners:
+        pl.semaphore_signal(barrier, inc=1, device_id=device, device_id_type=MESH)
+    pl.semaphore_wait(barrier, len(partners))
+
+    feats = [
+        send(x_ref, panel.at[rep], feat_sem, m, (flip(rep, m), blk))
+        for m in reversed(range(1, n_rep))
+    ]
+    for load in loads:
+        load.wait()
+
+    def place_row(row, carry):
+        at = pl.ds(pl.multiple_of(lax.rem(row, tiles_per_block) * side, side), side)
+        for col in range(col_tiles):
+            slot = slot_ref[row * col_tiles + col]
+            dense[lax.div(row, tiles_per_block), at, col * side:(col + 1) * side] = tiles[slot]
+        return carry
+
+    lax.fori_loop(0, n_blk * tiles_per_block, place_row, 0)
+    for copy in feats:
+        copy.wait_recv()
+
+    def forward(block):
+        source = panel[...].reshape(n_rep * rows, feat)
+        return jnp.dot(dense[block], source, preferred_element_type=f32)
+
+    def pair_step(mask):
+        block = flip(z, mask) * cores + 1 - core
+        pair_out[mask] = forward(block).astype(bf16)
+        return send(pair_out.at[mask], pair_in.at[mask], pair_sem, mask, pair)
+
+    order = list(reversed(range(n_z)))
+    pair_copies = {order[0]: pair_step(order[0])}
+    line_copies = {}
+    own_rows = None
+    for at, mask in enumerate(order):
+        if at + 1 < n_z:
+            pair_copies[order[at + 1]] = pair_step(order[at + 1])
+        total = forward(line(mask))
+        pair_copies[mask].wait_recv()
+        total = total + pair_in[mask].astype(f32)
+        if mask:
+            line_out[mask] = total.astype(bf16)
+            line_copies[mask] = send(
+                line_out.at[mask], line_in.at[mask], line_sem, mask, (rep, line(mask))
+            )
+        else:
+            own_rows = total
+    for mask in range(1, n_z):
+        line_copies[mask].wait_recv()
+        own_rows = own_rows + line_in[mask].astype(f32)
+
+    for k in range(tiles_per_block):
+        piece = slice(k * side, (k + 1) * side)
+        spread = jnp.broadcast_to(scale_ref[:, piece], (feat, side)).T
+        agg = (own_rows[piece] + spread * x_ref[piece, :].astype(f32)).astype(bf16)
+        agg_ref[piece, :] = agg
+        pre_act = jnp.dot(agg, w_ref[...], preferred_element_type=f32)
+        sigma = 1.0 / (1.0 + jnp.exp(-pre_act))
+        act_ref[piece, :] = (pre_act * sigma).astype(bf16)
+        rate = sigma * (1.0 + pre_act * (1.0 - sigma))
+        slope = (cot_ref[piece, :].astype(f32) * rate).astype(bf16)
+        slope_ref[piece, :] = slope
+        grads[blk, :, piece] = lax.dot_general(
+            w_ref[...], slope, (((1,), (1,)), ((), ())), preferred_element_type=f32
+        ).astype(bf16)
+
+    grad_line = {
+        m: send(grads.at[blk], grads.at[blk], grad_line_sem, m, (rep, line(m)))
+        for m in reversed(range(1, n_z))
+    }
+    grad_pair = {0: send(grads.at[blk], grads.at[blk], grad_pair_sem, 0, pair)}
+
+    w_part[...] = jnp.dot(agg_ref[...].T, slope_ref[...], preferred_element_type=f32)
+    share = feat // n_rep
+
+    def w_rows(place):
+        return pl.ds(pl.multiple_of(place * share, share), share)
+
+    w_rep = [
+        send(w_part.at[w_rows(flip(rep, m))], w_in.at[m], w_rep_sem, m, (flip(rep, m), blk))
+        for m in range(1, n_rep)
+    ]
+
+    def backward(block, first=False):
+        for q in range(n_rep):
+            term = jnp.dot(
+                grads[block], dense[block, :, q * rows:(q + 1) * rows], preferred_element_type=f32
+            )
+            sums[q] = term if first else sums[q] + term
+
+    backward(blk, True)
+    w_pair = None
+    w_line = []
+    for mask in range(n_z):
+        if mask:
+            grad_line[mask].wait_recv()
+            mine = grads.at[line(mask)]
+            grad_pair[mask] = send(mine, mine, grad_pair_sem, mask, pair)
+            backward(line(mask))
+        if mask == 1:
+            for copy in w_rep:
+                copy.wait_recv()
+            w_sum = w_part[w_rows(rep), :]
+            for m in range(1, n_rep):
+                w_sum = w_sum + w_in[m]
+            w_pair_out[...] = w_sum
+            w_pair = send(w_pair_out, w_pair_in, w_pair_sem, 0, pair)
+        grad_pair[mask].wait_recv()
+        other = flip(z, mask) * cores + 1 - core
+        if mask < n_z - 1:
+            backward(other)
+
+    w_pair.wait_recv()
+    w_line_out[...] = w_pair_out[...] + w_pair_in[...]
+    w_line = [
+        send(w_line_out, w_line_in.at[m], w_line_sem, m, (rep, line(m))) for m in range(1, n_z)
+    ]
+
+    def finished(block):
+        at = pl.ds(pl.multiple_of(block * rows, rows), rows)
+        return sums[block] + jnp.dot(
+            grads[other], dense[other, :, at], preferred_element_type=f32
+        )
+
+    col_copies = {}
+    for mask in reversed(range(1, n_rep)):
+        target = flip(rep, mask)
+        col_out[mask] = finished(target).astype(bf16)
+        col_copies[mask] = send(
+            col_out.at[mask], col_in.at[mask], col_sem, mask, (target, blk)
+        )
+    own_cols = finished(rep) + scale_ref[...] * grads[blk].astype(f32)
+
+    for copy in w_line:
+        copy.wait_recv()
+    w_all = w_line_out[...]
+    for m in range(1, n_z):
+        w_all = w_all + w_line_in[m]
+    wgrad_ref[...] = w_all * inv_root
+
+    for mask in range(1, n_rep):
+        col_copies[mask].wait_recv()
+        own_cols = own_cols + col_in[mask].astype(f32)
+    fgrad_ref[...] = own_cols.T.astype(bf16)
+    for copy in pending:
+        copy.wait_send()
+
+
+def fused_layer(
+    features, weight, cotangent, self_weight, block_rows, block_cols, block_counts, block_values
+):
+    n_rep = lax.axis_size("rep")
+    n_blk = lax.axis_size("blk")
+    n_z = n_blk // cores
+    _, rows, feat = features.shape
+    hidden = weight.shape[1]
+    cap, side = block_values.shape[2:4]
+    row_tiles = n_blk * rows // side
+    col_tiles = n_rep * rows // side
+    share = feat // n_rep
+    f32, bf16 = jnp.float32, jnp.bfloat16
+
+    slots = jnp.arange(cap, dtype=jnp.int32)
+    places = block_rows[0, 0] * col_tiles + block_cols[0, 0]
+    places = jnp.where(slots < block_counts[0, 0], places, -1)
+    grid = jnp.arange(row_tiles * col_tiles, dtype=jnp.int32)
+    slot_of = jnp.min(jnp.where(grid[:, None] == places[None, :], slots[None, :], cap), axis=1)
+
+    vmem = pl.BlockSpec(memory_space=pltpu.VMEM)
+    dma = pltpu.SemaphoreType.DMA
+    nodes = n_blk * n_rep * rows
+    macs = nodes * n_rep * rows * feat // n_rep * 2
+    activated, feature_grad, weight_grad = pl.pallas_call(
+        functools.partial(layer_kernel, n_rep, n_blk, 1.0 / math.sqrt(nodes)),
+        out_shape=(
+            jax.ShapeDtypeStruct((rows, hidden), bf16),
+            jax.ShapeDtypeStruct((rows, feat), bf16),
+            jax.ShapeDtypeStruct((share, hidden), f32),
+        ),
+        in_specs=[
+            pl.BlockSpec(memory_space=pltpu.SMEM), vmem, vmem, vmem, vmem,
+            pl.BlockSpec(memory_space=pl.ANY),
+        ],
+        out_specs=(vmem, vmem, vmem),
+        scratch_shapes=[
+            pltpu.VMEM((cap + 1, side, side), bf16),
+            pltpu.VMEM((n_blk, rows, n_rep * rows), bf16),
+            pltpu.VMEM((n_rep, rows, feat), bf16),
+            pltpu.VMEM((n_z, rows, feat), bf16),
+            pltpu.VMEM((n_z, rows, feat), bf16),
+            pltpu.VMEM((n_z, rows, feat), bf16),
+            pltpu.VMEM((n_z, rows, feat), bf16),
+            pltpu.VMEM((rows, feat), bf16),
+            pltpu.VMEM((rows, hidden), bf16),
+            pltpu.VMEM((n_blk, feat, rows), bf16),
+            pltpu.VMEM((n_rep, feat, rows), f32),
+            pltpu.VMEM((n_rep, feat, rows), bf16),
+            pltpu.VMEM((n_rep, feat, rows), bf16),
+            pltpu.VMEM((feat, hidden), f32),
+            pltpu.VMEM((n_rep, share, hidden), f32),
+            pltpu.VMEM((share, hidden), f32),
+            pltpu.VMEM((share, hidden), f32),
+            pltpu.VMEM((share, hidden), f32),
+            pltpu.VMEM((n_z, share, hidden), f32),
+            dma((load_parts,)),
+            dma((2, n_rep)),
+            dma((2, n_z)),
+            dma((2, n_z)),
+            dma((2, n_z)),
+            dma((2, n_z)),
+            dma((2, n_rep)),
+            dma((2, n_rep)),
+            dma((2, 1)),
+            dma((2, n_z)),
+        ],
+        compiler_params=pltpu.CompilerParams(
+            collective_id=0, has_side_effects=True, vmem_limit_bytes=vmem_bytes
+        ),
+        cost_estimate=pl.CostEstimate(
+            flops=2 * macs, bytes_accessed=cap * side * side * 2, transcendentals=rows * hidden
+        ),
+    )(slot_of, features[0], weight, cotangent[0], self_weight, block_values[0, 0])
+    return (activated[None], feature_grad[None], weight_grad)
+
+
+def streamed_layer(
     features, weight, cotangent, self_weight, block_rows, block_cols, block_counts, block_values
 ):
     rows_dev = features.shape[1]
@@ -98,6 +393,18 @@
     return (activated[None], feature_grad[None], weight_grad)
 
 
+def on_device(*arrays):
+    n_rep = lax.axis_size("rep")
+    n_blk = lax.axis_size("blk")
+    rows = arrays[0].shape[1]
+    n_z = n_blk // cores
+    powers = all(n & (n - 1) == 0 for n in (n_rep, n_z)) and n_z > 1 and n_blk % cores == 0
+    dense_bytes = 2 * n_blk * rows * n_rep * rows
+    if powers and dense_bytes <= dense_limit:
+        return fused_layer(*arrays)
+    return streamed_layer(*arrays)
+
+
 def solution(mesh):
     placed = (
         P("blk", "rep", None),

time: 372 us -> 60.2 us (0.16)
  waiting for transfers between devices: 254 us -> 0 us
  Pallas kernels: 0 us -> 52.3 us
  other arithmetic: 37.7 us -> 0.9 us
  local copies, waits for them, and re-layouts: 33.8 us -> 5.34 us
  matrix products: 14.8 us -> 0 us
  between operations: 14.5 us -> 1.3 us
  blocking collectives: 13.1 us -> 0 us
    reduce_scatter x2 -> x0, waiting for transfers between devices: 150 us -> none  [the longest x1 125 us: on_device(): lax.psum_scatter(forward_terms.astype(jnp.bfloat16), 'blk', scatter_dimen...]
    psum x1 -> x0, waiting for transfers between devices: 102 us -> none  [on_device(): weight_full = lax.psum(weight_part, ('rep', 'blk'))]
    pallas_call x0 -> x1, Pallas kernels: none -> 52.3 us  [fused_layer(): pl.pallas_call(functools.partial(layer_kernel, n_rep, n_blk, 1.0 / math.s...]
    scatter-add x6 -> x0, other arithmetic: 26.5 us -> none  [one_group(): return summed.at[landing].add(products * is_live[:, None, None])]
    dot_general x9 -> x0, matrix products: 14.8 us -> none  [the longest x3 5.91 us: one_group(): jnp.einsum('gji,gjf->gif', tile_block, picked, preferred_element_type=jnp...]
    gather x6 -> x0, local copies, waits for them, and re-layouts: 14 us -> none  [the longest x3 8.66 us: one_group(): picked = source[rows_here]]
    all_gather x1 -> x0, blocking collectives: 13.1 us -> none  [on_device(): panel = lax.all_gather(features, 'rep', axis=1, tiled=True)]
    unnamed x13 -> x11, local copies, waits for them, and re-layouts: 16.7 us -> 5.34 us
  transfers between devices with their start and end apart: 4 -> 0, of which waited for: 4 -> 0; matrix products, arithmetic and copies ran while one was open for 12% -> 0% of each run, Pallas kernels for 0% -> 0%
where the time goes in v1:
time: 60.2 us; the launch traced here: 59.9 us
  Pallas kernels  52.3 us (87%)
  local copies, waits for them, and re-layouts  5.34 us (9%)
  between operations  1.3 us (2%)
  other arithmetic  0.9 us (1%)
    pallas_call x1, Pallas kernels, fused_layer(): pl.pallas_call(functools.partial(layer_kernel, n_rep, n_blk, 1.0 / math.s...  52.3 us
    unnamed x11, local copies, waits for them, and re-layouts  5.34 us

profile of v1, /device:TPU:0, one launch (start us, length us, event | category | flops | bytes accessed | tf_op | source)
XLA Modules:
  0.0 59.9 jit_solution(16063713207341988974)
XLA Ops:
  1.3 0.7 %add_reduce_fusion = s32[384]{0:T(512)S(1)} fusion(s32[1,1,384]{2,1,0:T(1,128)} %param.13, s32[1,1,384]{2,1,0:T(1,128)} %param.12), kind=kLoop, calls=%fused_computation.4 | loop fusion | flops 768 | bytes 4608 | tf_op jit(solution)/shard_map/add | solution.py:280
  2.0 0.2 select_reduce_fusion.slot_ref
  2.2 0.0 copy-start
  2.2 0.9 %copy-done = bf16[1,512,256]{2,1,0:T(8,128)(2,1)S(1)} copy-done((bf16[1,512,256]{2,1,0:T(8,128)(2,1)S(1)}, bf16[1,512,256]{2,1,0:T(8,128)(2,1)}, u32[]{:S(2)}) %copy-start) | copy-done | bytes 262168
  3.1 0.0 copy-start.1
  3.1 0.9 %copy-done.1 = bf16[1,512,128]{2,1,0:T(8,128)(2,1)S(1)} copy-done((bf16[1,512,128]{2,1,0:T(8,128)(2,1)S(1)}, bf16[1,512,128]{2,1,0:T(8,128)(2,1)}, u32[]{:S(2)}) %copy-start.1) | copy-done | bytes 131096
  4.0 0.0 copy-start.2
  4.0 0.8 %copy-done.2 = bf16[128,256]{1,0:T(8,128)(2,1)S(1)} copy-done((bf16[128,256]{1,0:T(8,128)(2,1)S(1)}, bf16[128,256]{1,0:T(8,128)(2,1)}, u32[]{:S(2)}) %copy-start.2) | copy-done | bytes 65560
  4.9 0.0 copy-start.3
  4.9 0.7 %copy-done.3 = f32[1,512]{1,0:T(1,128)S(1)} copy-done((f32[1,512]{1,0:T(1,128)S(1)}, f32[1,512]{1,0:T(1,128)}, u32[]{:S(2)}) %copy-start.3) | copy-done | bytes 2072
  5.6 52.3 %shard_map.103 = (bf16[512,256]{1,0:T(8,128)(2,1)S(1)}, bf16[512,128]{1,0:T(8,128)(2,1)S(1)}, f32[32,256]{1,0:T(8,128)S(1)}) custom-call(s32[512]{0:T(512)S(1)} %select_reduce_fusion.slot_ref, bf16[512,128]{1,0:T(8,128)(2,1)S(1)} %bitcast.10, bf16[128,256]{1,0:T(8,128)(2,1)S(1)} %copy-done.2, bf16[512,256]{1,0:T(8,128)(2,1)S(1)} %bitcast.9, ...), custom_call_target="tpu_custom_call" | custom-call | flops 4294967296 | bytes 12582912 | tf_op jit(solution)/shard_map/pallas_call | solution.py:289
  57.9 0.7 %copy.15 = bf16[1,512,256]{2,1,0:T(8,128)(2,1)} copy(bf16[1,512,256]{2,1,0:T(8,128)(2,1)S(1)} %bitcast.7) | data formatting | bytes 524288
  58.6 0.7 %copy.16 = bf16[1,512,128]{2,1,0:T(8,128)(2,1)} copy(bf16[1,512,128]{2,1,0:T(8,128)(2,1)S(1)} %bitcast.8) | data formatting | bytes 262144
  59.3 0.6 %copy.17 = f32[32,256]{1,0:T(8,128)} copy(f32[32,256]{1,0:T(8,128)S(1)} %get-tuple-element.14) | data formatting | bytes 65536
  (1 shorter events, 0.0 us)
Async XLA Ops:
  2.2 1.0 %copy-start = (bf16[1,512,256]{2,1,0:T(8,128)(2,1)S(1)}, bf16[1,512,256]{2,1,0:T(8,128)(2,1)}, u32[]{:S(2)}) copy-start(bf16[1,512,256]{2,1,0:T(8,128)(2,1)} %param.10) | copy-start | bytes 786436
  3.1 0.9 %copy-start.1 = (bf16[1,512,128]{2,1,0:T(8,128)(2,1)S(1)}, bf16[1,512,128]{2,1,0:T(8,128)(2,1)}, u32[]{:S(2)}) copy-start(bf16[1,512,128]{2,1,0:T(8,128)(2,1)} %param.8) | copy-start | bytes 393220
  4.0 0.8 %copy-start.2 = (bf16[128,256]{1,0:T(8,128)(2,1)S(1)}, bf16[128,256]{1,0:T(8,128)(2,1)}, u32[]{:S(2)}) copy-start(bf16[128,256]{1,0:T(8,128)(2,1)} %w_ref.1) | copy-start | bytes 196612
  4.9 0.7 %copy-start.3 = (f32[1,512]{1,0:T(1,128)S(1)}, f32[1,512]{1,0:T(1,128)}, u32[]{:S(2)}) copy-start(f32[1,512]{1,0:T(1,128)} %scale_ref.1) | copy-start | bytes 6148

commit v2 on v1

--- a/solution.py
+++ b/solution.py
@@ -49,8 +49,10 @@
 
 cores = 2
 load_parts = 8
+halves = 2
+near, skip, far = 1, 2, 3
 dense_limit = 20 * 2**20
-vmem_bytes = 52 * 2**20
+vmem_bytes = 63 * 2**20
 MESH = pl.DeviceIdType.MESH
 
 
@@ -65,11 +67,12 @@
 
 def layer_kernel(
     n_rep, n_blk, inv_root,
-    slot_ref, x_ref, w_ref, cot_ref, scale_ref, values_ref,
+    slot_ref, x_hbm, w_hbm, cot_hbm, scale_ref, values_ref,
     act_ref, fgrad_ref, wgrad_ref,
-    tiles, dense, panel, pair_out, pair_in, line_out, line_in, agg_ref, slope_ref,
-    grads, sums, col_out, col_in, w_part, w_in, w_pair_out, w_pair_in, w_line_out, w_line_in,
-    tile_sem, feat_sem, pair_sem, line_sem, grad_line_sem, grad_pair_sem, col_sem,
+    tiles, dense, panel, w_ref, cot_ref, pair_out, pair_in, line_out, line_in, relay_in,
+    own_ref, agg_ref, slope_ref, grads, sums, col_out, col_in,
+    w_part, w_in, w_pair_out, w_pair_in, w_line_out, w_line_in,
+    load_sem, feat_sem, pair_sem, line_sem, grad_line_sem, grad_pair_sem, col_sem,
     w_rep_sem, w_pair_sem, w_line_sem,
 ):
     rep = lax.axis_index("rep")
@@ -77,8 +80,11 @@
     z = lax.div(blk, cores)
     core = lax.rem(blk, cores)
     n_z = n_blk // cores
+    inner = lax.rem(z + lax.div(z, 2), 2) == 1
+    end = lax.rem(z + lax.div(z, 2), 2) == 0
     cap, side, _ = values_ref.shape
-    rows, feat = x_ref.shape
+    _, rows, feat = panel.shape
+    half = rows // halves
     col_tiles = n_rep * rows // side
     tiles_per_block = rows // side
     f32, bf16 = jnp.float32, jnp.bfloat16
@@ -87,38 +93,56 @@
     def line(mask):
         return flip(z, mask) * cores + core
 
+    def line_device(mask):
+        return (rep, line(mask))
+
     pending = []
 
-    def send(source, target, sems, at, device):
-        copy = pltpu.make_async_remote_copy(
+    def ready(source, target, sems, at, device, arrives=None):
+        return pltpu.make_async_remote_copy(
             src_ref=source, dst_ref=target,
-            send_sem=sems.at[0, at], recv_sem=sems.at[1, at],
+            send_sem=sems.at[(0,) + at],
+            recv_sem=sems.at[(1,) + (at if arrives is None else arrives)],
             device_id=device, device_id_type=MESH,
         )
-        copy.start()
-        pending.append(copy)
+
+    def go(copy, only=None):
+        if only is None:
+            copy.start()
+        else:
+            pl.when(only)(copy.start)
+        pending.append((copy, only))
         return copy
 
+    def send(*args):
+        return go(ready(*args))
+
+    x_load = pltpu.make_async_copy(x_hbm, panel.at[rep], load_sem.at[load_parts])
+    x_load.start()
     part = cap // load_parts
     loads = []
     for k in range(load_parts):
         piece = pl.ds(k * part, part)
-        load = pltpu.make_async_copy(values_ref.at[piece], tiles.at[piece], tile_sem.at[k])
+        loads.append(
+            pltpu.make_async_copy(values_ref.at[piece], tiles.at[piece], load_sem.at[k])
+        )
+    loads.append(pltpu.make_async_copy(w_hbm, w_ref, load_sem.at[load_parts + 1]))
+    loads.append(pltpu.make_async_copy(cot_hbm, cot_ref, load_sem.at[load_parts + 2]))
+    for load in loads:
         load.start()
-        loads.append(load)
     tiles[cap] = jnp.zeros((side, side), bf16)
-    panel[rep] = x_ref[...]
 
     partners = [(flip(rep, m), blk) for m in range(1, n_rep)]
-    partners += [(rep, line(m)) for m in range(1, n_z)]
+    partners += [line_device(m) for m in range(1, n_z)]
     partners += [pair]
     barrier = pltpu.get_barrier_semaphore()
     for device in partners:
         pl.semaphore_signal(barrier, inc=1, device_id=device, device_id_type=MESH)
     pl.semaphore_wait(barrier, len(partners))
 
+    x_load.wait()
     feats = [
-        send(x_ref, panel.at[rep], feat_sem, m, (flip(rep, m), blk))
+        send(panel.at[rep], panel.at[rep], feat_sem, (m,), (flip(rep, m), blk))
         for m in reversed(range(1, n_rep))
     ]
     for load in loads:
@@ -135,107 +159,153 @@
     for copy in feats:
         copy.wait_recv()
 
-    def forward(block):
+    def forward(block, h):
         source = panel[...].reshape(n_rep * rows, feat)
-        return jnp.dot(dense[block], source, preferred_element_type=f32)
-
-    def pair_step(mask):
+        return jnp.dot(
+            dense[block, h * half:(h + 1) * half, :], source, preferred_element_type=f32
+        )
+
+    def pair_step(h, mask):
         block = flip(z, mask) * cores + 1 - core
-        pair_out[mask] = forward(block).astype(bf16)
-        return send(pair_out.at[mask], pair_in.at[mask], pair_sem, mask, pair)
-
-    order = list(reversed(range(n_z)))
-    pair_copies = {order[0]: pair_step(order[0])}
+        pair_out[h, mask] = forward(block, h).astype(bf16)
+        return send(
+            pair_out.at[h, mask], pair_in.at[h, mask], pair_sem, (h, mask), pair
+        )
+
+    steps = [(h, mask) for h in range(halves) for mask in (far, near, skip, 0)]
+    pair_copies = {steps[0]: pair_step(*steps[0])}
     line_copies = {}
-    own_rows = None
-    for at, mask in enumerate(order):
-        if at + 1 < n_z:
-            pair_copies[order[at + 1]] = pair_step(order[at + 1])
-        total = forward(line(mask))
-        pair_copies[mask].wait_recv()
-        total = total + pair_in[mask].astype(f32)
-        if mask:
-            line_out[mask] = total.astype(bf16)
-            line_copies[mask] = send(
-                line_out.at[mask], line_in.at[mask], line_sem, mask, (rep, line(mask))
+    for at, step in enumerate(steps):
+        h, mask = step
+        if at + 1 < len(steps):
+            pair_copies[steps[at + 1]] = pair_step(*steps[at + 1])
+        total = forward(line(mask), h)
+        pair_copies[step].wait_recv()
+        total = total + pair_in[h, mask].astype(f32)
+        if not mask:
+            own_ref[h] = total
+            continue
+        out = line_out.at[h, mask]
+        if mask == skip:
+            own_ref[h] = total
+            relayed = ready(out, relay_in.at[h], line_sem, (h, 0), line_device(near))
+
+            @pl.when(inner)
+            def _():
+                relayed.wait_recv()
+                own_ref[h] = own_ref[h] + relay_in[h].astype(f32)
+
+            total = own_ref[h]
+        line_out[h, mask] = total.astype(bf16)
+        direct = ready(out, line_in.at[h, mask], line_sem, (h, mask), line_device(mask))
+        line_copies[step] = direct
+        if mask == far:
+            go(direct, inner)
+            go(ready(out, relay_in.at[h], line_sem, (h, 0), line_device(near)), end)
+        else:
+            go(direct)
+
+    def own_layer(h):
+        own = own_ref[h]
+        for mask in (near, skip):
+            line_copies[h, mask].wait_recv()
+            own = own + line_in[h, mask].astype(f32)
+        own_ref[h] = own
+
+        @pl.when(inner)
+        def _():
+            line_copies[h, far].wait_recv()
+            own_ref[h] = own_ref[h] + line_in[h, far].astype(f32)
+
+        for k in range(half // side):
+            inside = slice(k * side, (k + 1) * side)
+            piece = slice(h * half + k * side, h * half + (k + 1) * side)
+            spread = jnp.broadcast_to(scale_ref[:, piece], (feat, side)).T
+            x_piece = panel[rep, piece, :].astype(f32)
+            agg = (own_ref[h, inside, :] + spread * x_piece).astype(bf16)
+            agg_ref[piece, :] = agg
+            pre_act = jnp.dot(agg, w_ref[...], preferred_element_type=f32)
+            sigma = 1.0 / (1.0 + jnp.exp(-pre_act))
+            act_ref[piece, :] = (pre_act * sigma).astype(bf16)
+            rate = sigma * (1.0 + pre_act * (1.0 - sigma))
+            slope = (cot_ref[piece, :].astype(f32) * rate).astype(bf16)
+            slope_ref[piece, :] = slope
+            grads[blk, h, :, inside] = lax.dot_general(
+                w_ref[...], slope, (((1,), (1,)), ((), ())), preferred_element_type=f32
+            ).astype(bf16)
+
+    grad_line = {}
+    grad_pair = {}
+
+    def send_own(h):
+        mine = grads.at[blk, h]
+        for mask in (skip, far, near):
+            copy = ready(mine, mine, grad_line_sem, (h, mask), line_device(mask))
+            grad_line[h, mask] = go(copy, inner if mask == far else None)
+        grad_pair[h, 0] = send(mine, mine, grad_pair_sem, (h, 0), pair)
+
+    def take(h, mask):
+        grad_line[h, mask].wait_recv()
+        theirs = grads.at[line(mask), h]
+        if mask == skip:
+            go(ready(theirs, theirs, grad_line_sem, (h, 0), line_device(near), (h, far)), inner)
+        grad_pair[h, mask] = send(theirs, theirs, grad_pair_sem, (h, mask), pair)
+
+    def backward(block, h, first=False):
+        for q in range(n_rep):
+            term = jnp.dot(
+                grads[block, h],
+                dense[block, h * half:(h + 1) * half, q * rows:(q + 1) * rows],
+                preferred_element_type=f32,
             )
-        else:
-            own_rows = total
-    for mask in range(1, n_z):
-        line_copies[mask].wait_recv()
-        own_rows = own_rows + line_in[mask].astype(f32)
-
-    for k in range(tiles_per_block):
-        piece = slice(k * side, (k + 1) * side)
-        spread = jnp.broadcast_to(scale_ref[:, piece], (feat, side)).T
-        agg = (own_rows[piece] + spread * x_ref[piece, :].astype(f32)).astype(bf16)
-        agg_ref[piece, :] = agg
-        pre_act = jnp.dot(agg, w_ref[...], preferred_element_type=f32)
-        sigma = 1.0 / (1.0 + jnp.exp(-pre_act))
-        act_ref[piece, :] = (pre_act * sigma).astype(bf16)
-        rate = sigma * (1.0 + pre_act * (1.0 - sigma))
-        slope = (cot_ref[piece, :].astype(f32) * rate).astype(bf16)
-        slope_ref[piece, :] = slope
-        grads[blk, :, piece] = lax.dot_general(
-            w_ref[...], slope, (((1,), (1,)), ((), ())), preferred_element_type=f32
-        ).astype(bf16)
-
-    grad_line = {
-        m: send(grads.at[blk], grads.at[blk], grad_line_sem, m, (rep, line(m)))
-        for m in reversed(range(1, n_z))
-    }
-    grad_pair = {0: send(grads.at[blk], grads.at[blk], grad_pair_sem, 0, pair)}
-
-    w_part[...] = jnp.dot(agg_ref[...].T, slope_ref[...], preferred_element_type=f32)
+            sums[q] = term if first else sums[q] + term
+
+    def other(mask):
+        return flip(z, mask) * cores + 1 - core
+
     share = feat // n_rep
 
     def w_rows(place):
         return pl.ds(pl.multiple_of(place * share, share), share)
 
+    for h in range(halves):
+        own_layer(h)
+        send_own(h)
+        piece = slice(h * half, (h + 1) * half)
+        term = jnp.dot(agg_ref[piece, :].T, slope_ref[piece, :], preferred_element_type=f32)
+        w_part[...] = term if h == 0 else w_part[...] + term
+        backward(blk, h, h == 0)
     w_rep = [
-        send(w_part.at[w_rows(flip(rep, m))], w_in.at[m], w_rep_sem, m, (flip(rep, m), blk))
+        send(w_part.at[w_rows(flip(rep, m))], w_in.at[m], w_rep_sem, (m,), (flip(rep, m), blk))
         for m in range(1, n_rep)
     ]
-
-    def backward(block, first=False):
-        for q in range(n_rep):
-            term = jnp.dot(
-                grads[block], dense[block, :, q * rows:(q + 1) * rows], preferred_element_type=f32
-            )
-            sums[q] = term if first else sums[q] + term
-
-    backward(blk, True)
-    w_pair = None
-    w_line = []
-    for mask in range(n_z):
-        if mask:
-            grad_line[mask].wait_recv()
-            mine = grads.at[line(mask)]
-            grad_pair[mask] = send(mine, mine, grad_pair_sem, mask, pair)
-            backward(line(mask))
-        if mask == 1:
+    for h in range(halves):
+        grad_pair[h, 0].wait_recv()
+        backward(other(0), h)
+
+    arrivals = [(h, mask) for h in range(halves) for mask in (skip, near, far)]
+    for at, (h, mask) in enumerate(arrivals):
+        take(h, mask)
+        backward(line(mask), h)
+        if at == 1:
             for copy in w_rep:
                 copy.wait_recv()
             w_sum = w_part[w_rows(rep), :]
             for m in range(1, n_rep):
                 w_sum = w_sum + w_in[m]
             w_pair_out[...] = w_sum
-            w_pair = send(w_pair_out, w_pair_in, w_pair_sem, 0, pair)
-        grad_pair[mask].wait_recv()
-        other = flip(z, mask) * cores + 1 - core
-        if mask < n_z - 1:
-            backward(other)
-
-    w_pair.wait_recv()
-    w_line_out[...] = w_pair_out[...] + w_pair_in[...]
-    w_line = [
-        send(w_line_out, w_line_in.at[m], w_line_sem, m, (rep, line(m))) for m in range(1, n_z)
-    ]
+            w_pair = send(w_pair_out, w_pair_in, w_pair_sem, (0,), pair)
+        grad_pair[h, mask].wait_recv()
+        if at + 1 < len(arrivals):
+            backward(other(mask), h)
+
+    h, mask = arrivals[-1]
+    last = other(mask)
 
     def finished(block):
         at = pl.ds(pl.multiple_of(block * rows, rows), rows)
         return sums[block] + jnp.dot(
-            grads[other], dense[other, :, at], preferred_element_type=f32
+            grads[last, h], dense[last, h * half:(h + 1) * half, at], preferred_element_type=f32
         )
 
     col_copies = {}
@@ -243,9 +313,17 @@
         target = flip(rep, mask)
         col_out[mask] = finished(target).astype(bf16)
         col_copies[mask] = send(
-            col_out.at[mask], col_in.at[mask], col_sem, mask, (target, blk)
-        )
-    own_cols = finished(rep) + scale_ref[...] * grads[blk].astype(f32)
+            col_out.at[mask], col_in.at[mask], col_sem, (mask,), (target, blk)
+        )
+
+    w_pair.wait_recv()
+    w_line_out[...] = w_pair_out[...] + w_pair_in[...]
+    w_line = [
+        send(w_line_out, w_line_in.at[m], w_line_sem, (m,), line_device(m))
+        for m in range(1, n_z)
+    ]
+    own_grads = jnp.concatenate([grads[blk, h] for h in range(halves)], axis=1)
+    own_cols = finished(rep) + scale_ref[...] * own_grads.astype(f32)
 
     for copy in w_line:
         copy.wait_recv()
@@ -258,8 +336,11 @@
         col_copies[mask].wait_recv()
         own_cols = own_cols + col_in[mask].astype(f32)
     fgrad_ref[...] = own_cols.T.astype(bf16)
-    for copy in pending:
-        copy.wait_send()
+    for copy, only in pending:
+        if only is None:
+            copy.wait_send()
+        else:
+            pl.when(only)(copy.wait_send)
 
 
 def fused_layer(
@@ -283,6 +364,8 @@
     slot_of = jnp.min(jnp.where(grid[:, None] == places[None, :], slots[None, :], cap), axis=1)
 
     vmem = pl.BlockSpec(memory_space=pltpu.VMEM)
+    hbm = pl.BlockSpec(memory_space=pltpu.HBM)
+    half = rows // halves
     dma = pltpu.SemaphoreType.DMA
     nodes = n_blk * n_rep * rows
     macs = nodes * n_rep * rows * feat // n_rep * 2
@@ -294,21 +377,24 @@
             jax.ShapeDtypeStruct((share, hidden), f32),
         ),
         in_specs=[
-            pl.BlockSpec(memory_space=pltpu.SMEM), vmem, vmem, vmem, vmem,
-            pl.BlockSpec(memory_space=pl.ANY),
+            pl.BlockSpec(memory_space=pltpu.SMEM), hbm, hbm, hbm, vmem, hbm,
         ],
         out_specs=(vmem, vmem, vmem),
         scratch_shapes=[
             pltpu.VMEM((cap + 1, side, side), bf16),
             pltpu.VMEM((n_blk, rows, n_rep * rows), bf16),
             pltpu.VMEM((n_rep, rows, feat), bf16),
-            pltpu.VMEM((n_z, rows, feat), bf16),
-            pltpu.VMEM((n_z, rows, feat), bf16),
-            pltpu.VMEM((n_z, rows, feat), bf16),
-            pltpu.VMEM((n_z, rows, feat), bf16),
+            pltpu.VMEM((feat, hidden), bf16),
+            pltpu.VMEM((rows, hidden), bf16),
+            pltpu.VMEM((halves, n_z, half, feat), bf16),
+            pltpu.VMEM((halves, n_z, half, feat), bf16),
+            pltpu.VMEM((halves, n_z, half, feat), bf16),
+            pltpu.VMEM((halves, n_z, half, feat), bf16),
+            pltpu.VMEM((halves, half, feat), bf16),
+            pltpu.VMEM((halves, half, feat), f32),
             pltpu.VMEM((rows, feat), bf16),
             pltpu.VMEM((rows, hidden), bf16),
-            pltpu.VMEM((n_blk, feat, rows), bf16),
+            pltpu.VMEM((n_blk, halves, feat, half), bf16),
             pltpu.VMEM((n_rep, feat, rows), f32),
             pltpu.VMEM((n_rep, feat, rows), bf16),
             pltpu.VMEM((n_rep, feat, rows), bf16),
@@ -318,12 +404,12 @@
             pltpu.VMEM((share, hidden), f32),
             pltpu.VMEM((share, hidden), f32),
             pltpu.VMEM((n_z, share, hidden), f32),
-            dma((load_parts,)),
+            dma((load_parts + 3,)),
             dma((2, n_rep)),
-            dma((2, n_z)),
-            dma((2, n_z)),
-            dma((2, n_z)),
-            dma((2, n_z)),
+            dma((2, halves, n_z)),
+            dma((2, halves, n_z)),
+            dma((2, halves, n_z)),
+            dma((2, halves, n_z)),
             dma((2, n_rep)),
             dma((2, n_rep)),
             dma((2, 1)),
@@ -398,9 +484,9 @@
     n_blk = lax.axis_size("blk")
     rows = arrays[0].shape[1]
     n_z = n_blk // cores
-    powers = all(n & (n - 1) == 0 for n in (n_rep, n_z)) and n_z > 1 and n_blk % cores == 0
+    fits = n_z == 4 and n_blk % cores == 0 and n_rep & (n_rep - 1) == 0
     dense_bytes = 2 * n_blk * rows * n_rep * rows
-    if powers and dense_bytes <= dense_limit:
+    if fits and dense_bytes <= dense_limit:
         return fused_layer(*arrays)
     return streamed_layer(*arrays)
 

time: 60.2 us -> 56.9 us (0.945)
  Pallas kernels: 52.3 us -> 49.3 us
  local copies, waits for them, and re-layouts: 5.34 us -> 4.61 us
    pallas_call x1, Pallas kernels: 52.3 us -> 49.3 us  [fused_layer(): pl.pallas_call(functools.partial(layer_kernel, n_rep, n_blk, 1.0 / math.s...]
    unnamed x11 -> x3, local copies, waits for them, and re-layouts: 5.34 us -> 4.61 us
where the time goes in v2:
time: 56.9 us; the launch traced here: 56.6 us
  Pallas kernels  49.3 us (87%)
  local copies, waits for them, and re-layouts  4.61 us (8%)
  other arithmetic  1.48 us (3%)
  between operations  1.29 us (2%)
    pallas_call x1, Pallas kernels, fused_layer(): pl.pallas_call(functools.partial(layer_kernel, n_rep, n_blk, 1.0 / math.s...  49.3 us
    unnamed x3, local copies, waits for them, and re-layouts  4.61 us

profile of v2, /device:TPU:0, one launch (start us, length us, event | category | flops | bytes accessed | tf_op | source)
XLA Modules:
  0.0 56.6 jit_solution(2490348187807981769)
XLA Ops:
  1.3 0.7 %add_reduce_fusion = s32[384]{0:T(512)S(1)} fusion(s32[1,1,384]{2,1,0:T(1,128)} %param.13, s32[1,1,384]{2,1,0:T(1,128)} %param.12), kind=kLoop, calls=%fused_computation.4 | loop fusion | flops 768 | bytes 4608 | tf_op jit(solution)/shard_map/add | solution.py:361
  2.0 0.8 %select_reduce_fusion.slot_ref = s32[512]{0:T(512)} fusion(s32[384]{0:T(512)S(1)} %fusion), kind=kLoop, calls=%fused_computation | loop fusion | flops 589312 | bytes 3584 | tf_op jit(solution)/shard_map/reduce_min | solution.py:364
  2.8 49.3 %shard_map.103 = (bf16[512,256]{1,0:T(8,128)(2,1)}, bf16[512,128]{1,0:T(8,128)(2,1)}, f32[32,256]{1,0:T(8,128)}) custom-call(s32[512]{0:T(512)} %select_reduce_fusion.slot_ref, bf16[512,128]{1,0:T(8,128)(2,1)} %bitcast.11, bf16[128,256]{1,0:T(8,128)(2,1)} %w_hbm.1, bf16[512,256]{1,0:T(8,128)(2,1)} %bitcast.10, f32[1,512]{1,0:T(1,128)} %scale_ref.1, ...), custom_call_target="tpu_custom_call" | custom-call | flops 4294967296 | bytes 12582912 | tf_op jit(solution)/shard_map/pallas_call | solution.py:372
  52.0 1.7 %copy.15 = bf16[1,512,256]{2,1,0:T(8,128)(2,1)} copy(bf16[1,512,256]{2,1,0:T(8,128)(2,1)} %bitcast.7) | data formatting | bytes 524288
  53.7 1.6 %copy.16 = bf16[1,512,128]{2,1,0:T(8,128)(2,1)} copy(bf16[1,512,128]{2,1,0:T(8,128)(2,1)} %bitcast.8) | data formatting | bytes 262144
  55.3 1.4 %copy.17 = f32[32,256]{1,0:T(8,128)} copy(f32[32,256]{1,0:T(8,128)} %get-tuple-element.14) | data formatting | bytes 65536
  (1 shorter events, 0.0 us)

commit v3 on v2

--- a/solution.py
+++ b/solution.py
@@ -67,9 +67,9 @@
 
 def layer_kernel(
     n_rep, n_blk, inv_root,
-    slot_ref, x_hbm, w_hbm, cot_hbm, scale_ref, values_ref,
+    rows_ref, cols_ref, count_ref, x_hbm, w_hbm, cot_hbm, scale_ref, values_ref,
     act_ref, fgrad_ref, wgrad_ref,
-    tiles, dense, panel, w_ref, cot_ref, pair_out, pair_in, line_out, line_in, relay_in,
+    slot_map, slot_ref, tiles, dense, panel, w_ref, cot_ref, pair_out, pair_in, line_out, line_in, relay_in,
     own_ref, agg_ref, slope_ref, grads, sums, col_out, col_in,
     w_part, w_in, w_pair_out, w_pair_in, w_line_out, w_line_in,
     load_sem, feat_sem, pair_sem, line_sem, grad_line_sem, grad_pair_sem, col_sem,
@@ -145,21 +145,48 @@
         send(panel.at[rep], panel.at[rep], feat_sem, (m,), (flip(rep, m), blk))
         for m in reversed(range(1, n_rep))
     ]
+
+    lanes = slot_map.shape[1]
+    places = lax.broadcasted_iota(jnp.int32, slot_map.shape, 0) * lanes
+    places = places + lax.broadcasted_iota(jnp.int32, slot_map.shape, 1)
+    count = count_ref[0, 0]
+
+    def name_place(slot, named):
+        place = rows_ref[0, slot] * col_tiles + cols_ref[0, slot]
+        place = jnp.where(slot < count, place, -1)
+        return jnp.where(places == place, slot, named)
+
+    slot_map[...] = lax.fori_loop(
+        0, cap, name_place, jnp.full(slot_map.shape, cap, jnp.int32), unroll=8
+    )
+    map_copy = pltpu.make_async_copy(slot_map, slot_ref, load_sem.at[load_parts + 3])
+    map_copy.start()
+    map_copy.wait()
     for load in loads:
         load.wait()
 
-    def place_row(row, carry):
-        at = pl.ds(pl.multiple_of(lax.rem(row, tiles_per_block) * side, side), side)
-        for col in range(col_tiles):
-            slot = slot_ref[row * col_tiles + col]
-            dense[lax.div(row, tiles_per_block), at, col * side:(col + 1) * side] = tiles[slot]
+    def place(block, h):
+        def place_row(k, carry):
+            first = (block * tiles_per_block + h * (half // side) + k) * col_tiles
+            at = pl.ds(pl.multiple_of(h * half + k * side, side), side)
+            for col in range(col_tiles):
+                slot = slot_ref[lax.div(first, lanes), lax.rem(first, lanes) + col]
+                dense[block, at, col * side:(col + 1) * side] = tiles[slot]
+            return carry
+
+        lax.fori_loop(0, half // side, place_row, 0)
+
+    def place_block(block, carry):
+        place(block, 0)
         return carry
 
-    lax.fori_loop(0, n_blk * tiles_per_block, place_row, 0)
+    lax.fori_loop(0, n_blk, place_block, 0)
     for copy in feats:
         copy.wait_recv()
 
     def forward(block, h):
+        if h:
+            place(block, h)
         source = panel[...].reshape(n_rep * rows, feat)
         return jnp.dot(
             dense[block, h * half:(h + 1) * half, :], source, preferred_element_type=f32
@@ -343,6 +370,15 @@
             pl.when(only)(copy.wait_send)
 
 
+def hand_over(a_ref, b_ref, c_ref, a_out, b_out, c_out, sems):
+    pairs = ((a_ref, a_out), (b_ref, b_out), (c_ref, c_out))
+    copies = [pltpu.make_async_copy(p, q, sems.at[k]) for k, (p, q) in enumerate(pairs)]
+    for copy in copies:
+        copy.start()
+    for copy in copies:
+        copy.wait()
+
+
 def fused_layer(
     features, weight, cotangent, self_weight, block_rows, block_cols, block_counts, block_values
 ):
@@ -357,14 +393,11 @@
     share = feat // n_rep
     f32, bf16 = jnp.float32, jnp.bfloat16
 
-    slots = jnp.arange(cap, dtype=jnp.int32)
-    places = block_rows[0, 0] * col_tiles + block_cols[0, 0]
-    places = jnp.where(slots < block_counts[0, 0], places, -1)
-    grid = jnp.arange(row_tiles * col_tiles, dtype=jnp.int32)
-    slot_of = jnp.min(jnp.where(grid[:, None] == places[None, :], slots[None, :], cap), axis=1)
-
+    map_lanes = 128
+    map_rows = row_tiles * col_tiles // map_lanes
     vmem = pl.BlockSpec(memory_space=pltpu.VMEM)
     hbm = pl.BlockSpec(memory_space=pltpu.HBM)
+    smem = pl.BlockSpec(memory_space=pltpu.SMEM)
     half = rows // halves
     dma = pltpu.SemaphoreType.DMA
     nodes = n_blk * n_rep * rows
@@ -377,10 +410,12 @@
             jax.ShapeDtypeStruct((share, hidden), f32),
         ),
         in_specs=[
-            pl.BlockSpec(memory_space=pltpu.SMEM), hbm, hbm, hbm, vmem, hbm,
+            smem, smem, smem, hbm, hbm, hbm, vmem, hbm,
         ],
         out_specs=(vmem, vmem, vmem),
         scratch_shapes=[
+            pltpu.VMEM((map_rows, map_lanes), jnp.int32),
+            pltpu.SMEM((map_rows, map_lanes), jnp.int32),
             pltpu.VMEM((cap + 1, side, side), bf16),
             pltpu.VMEM((n_blk, rows, n_rep * rows), bf16),
             pltpu.VMEM((n_rep, rows, feat), bf16),
@@ -404,7 +439,7 @@
             pltpu.VMEM((share, hidden), f32),
             pltpu.VMEM((share, hidden), f32),
             pltpu.VMEM((n_z, share, hidden), f32),
-            dma((load_parts + 3,)),
+            dma((load_parts + 4,)),
             dma((2, n_rep)),
             dma((2, halves, n_z)),
             dma((2, halves, n_z)),
@@ -421,8 +456,19 @@
         cost_estimate=pl.CostEstimate(
             flops=2 * macs, bytes_accessed=cap * side * side * 2, transcendentals=rows * hidden
         ),
-    )(slot_of, features[0], weight, cotangent[0], self_weight, block_values[0, 0])
-    return (activated[None], feature_grad[None], weight_grad)
+    )(
+        block_rows[0], block_cols[0], block_counts,
+        features[0], weight, cotangent[0], self_weight, block_values[0, 0],
+    )
+    results = (activated[None], feature_grad[None], weight_grad)
+    return pl.pallas_call(
+        hand_over,
+        out_shape=tuple(jax.ShapeDtypeStruct(r.shape, r.dtype) for r in results),
+        in_specs=[hbm] * 3,
+        out_specs=(hbm,) * 3,
+        scratch_shapes=[dma((3,))],
+        compiler_params=pltpu.CompilerParams(vmem_limit_bytes=vmem_bytes),
+    )(*results)
 
 
 def streamed_layer(
@@ -485,6 +531,8 @@
     rows = arrays[0].shape[1]
     n_z = n_blk // cores
     fits = n_z == 4 and n_blk % cores == 0 and n_rep & (n_rep - 1) == 0
+    side = arrays[-1].shape[-1]
+    fits = fits and 128 % (n_rep * rows // side) == 0
     dense_bytes = 2 * n_blk * rows * n_rep * rows
     if fits and dense_bytes <= dense_limit:
         return fused_layer(*arrays)

time: 56.9 us -> 66.9 us (1.18)
  Pallas kernels: 49.3 us -> 65.3 us
  local copies, waits for them, and re-layouts: 4.61 us -> 0 us
  other arithmetic: 1.48 us -> 0 us
    pallas_call x0 -> x1, Pallas kernels: none -> 14 us  [fused_layer(): pl.pallas_call(hand_over, out_shape=tuple((jax.ShapeDtypeStruct(r.shape,...]
    unnamed x3 -> x0, local copies, waits for them, and re-layouts: 4.61 us -> none
    pallas_call x1, Pallas kernels: 49.3 us -> 51.2 us  [fused_layer(): pl.pallas_call(functools.partial(layer_kernel, n_rep, n_blk, 1.0 / math.s...]
    reduce_min x1 -> x0, other arithmetic: 0.75 us -> none  [fused_layer(): jnp.min(jnp.where(grid[:, None] == places[None, :], slots[None, :], cap),...]
    add x1 -> x0, other arithmetic: 0.72 us -> none  [fused_layer(): places = block_rows[0, 0] * col_tiles + block_cols[0, 0]]
where the time goes in v3:
time: 66.9 us; the launch traced here: 66.7 us
  Pallas kernels  65.3 us (98%)
  between operations  1.45 us (2%)
    pallas_call x1, Pallas kernels, fused_layer(): pl.pallas_call(functools.partial(layer_kernel, n_rep, n_blk, 1.0 / math.s...  51.2 us
    pallas_call x1, Pallas kernels, fused_layer(): pl.pallas_call(hand_over, out_shape=tuple((jax.ShapeDtypeStruct(r.shape,...  14 us

profile of v3, /device:TPU:0, one launch (start us, length us, event | category | flops | bytes accessed | tf_op | source)
XLA Modules:
  0.0 66.7 jit_solution(181472665834503034)
XLA Ops:
  1.3 51.2 %shard_map.103 = (bf16[512,256]{1,0:T(8,128)(2,1)}, bf16[512,128]{1,0:T(8,128)(2,1)}, f32[32,256]{1,0:T(8,128)}) custom-call(s32[1,384]{1,0:T(1,128)} %bitcast.12, s32[1,384]{1,0:T(1,128)} %bitcast.13, s32[1,1]{1,0:T(1,128)S(6)} %copy.11.count_ref, bf16[512,128]{1,0:T(8,128)(2,1)} %bitcast.11, bf16[128,256]{1,0:T(8,128)(2,1)} %w_hbm.1, ...), custom_call_target="tpu_custom_call" | custom-call | flops 4294967296 | bytes 12582912 | tf_op jit(solution)/shard_map/pallas_call | solution.py:405
  52.5 14.0 %shard_map.104 = (bf16[1,512,256]{2,1,0:T(8,128)(2,1)}, bf16[1,512,128]{2,1,0:T(8,128)(2,1)}, f32[32,256]{1,0:T(8,128)}) custom-call(bf16[1,512,256]{2,1,0:T(8,128)(2,1)} %bitcast.7, bf16[1,512,128]{2,1,0:T(8,128)(2,1)} %bitcast.8, f32[32,256]{1,0:T(8,128)} %get-tuple-element.8.c_ref), custom_call_target="tpu_custom_call" | custom-call | tf_op jit(solution)/shard_map/pallas_call | solution.py:464

commit v4 on v3

--- a/solution.py
+++ b/solution.py
@@ -52,7 +52,7 @@
 halves = 2
 near, skip, far = 1, 2, 3
 dense_limit = 20 * 2**20
-vmem_bytes = 63 * 2**20
+vmem_bytes = 60 * 2**20
 MESH = pl.DeviceIdType.MESH
 
 
@@ -370,15 +370,6 @@
             pl.when(only)(copy.wait_send)
 
 
-def hand_over(a_ref, b_ref, c_ref, a_out, b_out, c_out, sems):
-    pairs = ((a_ref, a_out), (b_ref, b_out), (c_ref, c_out))
-    copies = [pltpu.make_async_copy(p, q, sems.at[k]) for k, (p, q) in enumerate(pairs)]
-    for copy in copies:
-        copy.start()
-    for copy in copies:
-        copy.wait()
-
-
 def fused_layer(
     features, weight, cotangent, self_weight, block_rows, block_cols, block_counts, block_values
 ):
@@ -405,9 +396,9 @@
     activated, feature_grad, weight_grad = pl.pallas_call(
         functools.partial(layer_kernel, n_rep, n_blk, 1.0 / math.sqrt(nodes)),
         out_shape=(
-            jax.ShapeDtypeStruct((rows, hidden), bf16),
-            jax.ShapeDtypeStruct((rows, feat), bf16),
-            jax.ShapeDtypeStruct((share, hidden), f32),
+            pltpu.VMEM((rows, hidden), bf16),
+            pltpu.VMEM((rows, feat), bf16),
+            pltpu.VMEM((share, hidden), f32),
         ),
         in_specs=[
             smem, smem, smem, hbm, hbm, hbm, vmem, hbm,
@@ -460,15 +451,7 @@
         block_rows[0], block_cols[0], block_counts,
         features[0], weight, cotangent[0], self_weight, block_values[0, 0],
     )
-    results = (activated[None], feature_grad[None], weight_grad)
-    return pl.pallas_call(
-        hand_over,
-        out_shape=tuple(jax.ShapeDtypeStruct(r.shape, r.dtype) for r in results),
-        in_specs=[hbm] * 3,
-        out_specs=(hbm,) * 3,
-        scratch_shapes=[dma((3,))],
-        compiler_params=pltpu.CompilerParams(vmem_limit_bytes=vmem_bytes),
-    )(*results)
+    return (activated[None], feature_grad[None], weight_grad)
 
 
 def streamed_layer(

time: 66.9 us -> 53.9 us (0.81)
  Pallas kernels: 65.3 us -> 50.5 us
  local copies, waits for them, and re-layouts: 0 us -> 1.97 us
    pallas_call x1 -> x0, Pallas kernels: 14 us -> none  [fused_layer(): pl.pallas_call(hand_over, out_shape=tuple((jax.ShapeDtypeStruct(r.shape,...]
    unnamed x0 -> x3, local copies, waits for them, and re-layouts: none -> 1.97 us
    pallas_call x1, Pallas kernels: 51.2 us -> 50.5 us  [fused_layer(): pl.pallas_call(functools.partial(layer_kernel, n_rep, n_blk, 1.0 / math.s...]
where the time goes in v4:
time: 53.9 us; the launch traced here: 53.7 us
  Pallas kernels  50.5 us (94%)
  local copies, waits for them, and re-layouts  1.97 us (4%)
  between operations  1.29 us (2%)
    pallas_call x1, Pallas kernels, fused_layer(): pl.pallas_call(functools.partial(layer_kernel, n_rep, n_blk, 1.0 / math.s...  50.5 us
    unnamed x3, local copies, waits for them, and re-layouts  1.97 us

profile of v4, /device:TPU:0, one launch (start us, length us, event | category | flops | bytes accessed | tf_op | source)
XLA Modules:
  0.0 53.7 jit_solution(2630780275674199468)
XLA Ops:
  1.3 50.5 %shard_map.103 = (bf16[512,256]{1,0:T(8,128)(2,1)S(1)}, bf16[512,128]{1,0:T(8,128)(2,1)S(1)}, f32[32,256]{1,0:T(8,128)S(1)}) custom-call(s32[1,384]{1,0:T(1,128)} %bitcast.12, s32[1,384]{1,0:T(1,128)} %bitcast.13, s32[1,1]{1,0:T(1,128)S(6)} %copy.17.count_ref, bf16[512,128]{1,0:T(8,128)(2,1)} %bitcast.11, bf16[128,256]{1,0:T(8,128)(2,1)} %w_hbm.1, ...), custom_call_target="tpu_custom_call" | custom-call | flops 4294967296 | bytes 12582912 | tf_op jit(solution)/shard_map/pallas_call | solution.py:396
  51.8 0.7 %copy.14 = bf16[1,512,256]{2,1,0:T(8,128)(2,1)} copy(bf16[1,512,256]{2,1,0:T(8,128)(2,1)S(1)} %bitcast.7) | data formatting | bytes 524288
  52.5 0.7 %copy.15 = bf16[1,512,128]{2,1,0:T(8,128)(2,1)} copy(bf16[1,512,128]{2,1,0:T(8,128)(2,1)S(1)} %bitcast.8) | data formatting | bytes 262144
  53.1 0.6 %copy.16 = f32[32,256]{1,0:T(8,128)} copy(f32[32,256]{1,0:T(8,128)S(1)} %get-tuple-element.11) | data formatting | bytes 65536
